TPU v7x, 512 devices: a whole 4x4x16 slice. The times are simulated.
512 devices in a mesh: batch: 8 (over z_lo, core), item: 64 (over x, z_hi, y).
Axes of the slice: x: 4, y: 4, z: 16 (z_hi: 4, z_lo: 4; z = z_hi * 4 + z_lo), core: 2. Of those that a mesh axis runs over, the one named last changes fastest.
Arguments:
- hidden: bfloat16 [4096, 256], P(('batch', 'item')), may hold values from -80 to 80
- item_table: bfloat16 [491520, 256], P('item'), may hold values from -0.75 to 0.75
- bucket_blocks: int32 [64, 128], P('batch'), may hold values from 0 to 959, as said below
- targets: int32 [4096], P('batch'), may hold values from 0 to 491519, as said below
- row_weight: float32 [4096], P('batch'), may hold values from 0.5 to 1.5
Outputs:
- row_loss: float32 [4096], P(('batch', 'item'))
- grad_hidden: bfloat16 [4096, 256], P(('batch', 'item'))
- grad_table: bfloat16 [256, 491520], P('batch', 'item')
Inputs may be any that keep to these rules, and one draw needn't show every extreme that they name: `bucket_blocks`: each row lists 128 distinct blocks; block j lies on item index j // 15; at most 8 blocks of a row lie on one item index, and in every row some index holds exactly 8. targets[r] lies in a block listed in row r // 64 of bucket_blocks.
All inputs are finite; a program needn't handle non-finite values.
Results may differ from a plain program's by a relative error of at most 0.0055.
Values may be sent and summed in bfloat16 or wider, within the bound.
A program may use at most 128 MiB of HBM per device.

v0:
```python
import jax
import jax.numpy as jnp
from jax import lax
from jax.sharding import PartitionSpec as P

BLK = 512
MOST = 8


NEGATIVE = -1e30


def slot_layout(block_lists, owner_index, per_device, capacity):
    local_ids = block_lists - owner_index * per_device
    is_owned = (local_ids >= 0) & (local_ids < per_device)
    placed = jnp.cumsum(is_owned.astype(jnp.int32), axis=1) - 1
    picked = is_owned[:, :, None] & (
        placed[:, :, None] == jnp.arange(capacity, dtype=jnp.int32)[None, None, :]
    )
    slot_block = jnp.sum(jnp.where(picked, local_ids[:, :, None], 0), axis=1)
    slot_valid = jnp.any(picked, axis=1)
    return (slot_block, slot_valid)


def bucket_scores(
    bucketed_rows, item_table, block_lists, targets, owner_index, capacity, block_width
):
    per_device = item_table.shape[0] // block_width
    buckets, bucket_rows, features = bucketed_rows.shape
    slot_block, slot_valid = slot_layout(block_lists, owner_index, per_device, capacity)
    block_panels = item_table.reshape(per_device, block_width, features)[slot_block]
    logit_values = jnp.einsum(
        "ahr,anor->ahno", bucketed_rows, block_panels, preferred_element_type=jnp.float32
    )
    live_mask = jnp.broadcast_to(slot_valid[:, None, :, None], logit_values.shape)
    logit_values = jnp.where(live_mask, logit_values, NEGATIVE)
    aimed_items = targets.reshape(buckets, bucket_rows)
    target_block = aimed_items // block_width - owner_index * per_device
    offsets = aimed_items % block_width
    target_mask = (
        live_mask
        & (slot_block[:, None, :, None] == target_block[:, :, None, None])
        & (
            jnp.arange(block_width, dtype=jnp.int32)[None, None, None, :]
            == offsets[:, :, None, None]
        )
    )
    return (block_panels, slot_block, slot_valid, logit_values, live_mask, target_mask)


def coefficients(logit_values, live_mask, target_mask, row_max, row_total, weights):
    chance = jnp.exp(logit_values - row_max[:, :, None, None]) / row_total[:, :, None, None]
    scaled = weights[:, :, None, None] * (chance - target_mask.astype(jnp.float32))
    return jnp.where(live_mask, scaled, 0.0).astype(jnp.bfloat16)


def spread_blocks(softmax_factor, slot_block, slot_valid, per_device):
    select = (
        slot_valid[:, :, None]
        & (slot_block[:, :, None] == jnp.arange(per_device, dtype=jnp.int32)[None, None, :])
    ).astype(jnp.bfloat16)
    return jnp.einsum(
        "bse,bqsi->bqei", select, softmax_factor, preferred_element_type=jnp.float32
    ).astype(jnp.bfloat16)


def on_device(hidden, item_table, bucket_blocks, targets, row_weight):
    owner_index = lax.axis_index("item")
    block_width = BLK
    capacity = MOST
    gathered = lax.all_gather(hidden, "item", axis=0, tiled=True)
    features = gathered.shape[1]
    buckets = bucket_blocks.shape[0]
    bucketed_rows = gathered.reshape(buckets, -1, features)
    weights = row_weight.reshape(buckets, -1)
    per_device = item_table.shape[0] // block_width
    block_panels, slot_block, slot_valid, logit_values, live_mask, target_mask = bucket_scores(
        bucketed_rows, item_table, bucket_blocks, targets, owner_index, capacity, block_width
    )
    local_max = jnp.max(logit_values, axis=(2, 3))
    row_max = lax.pmax(local_max, "item")
    local_total = jnp.sum(
        jnp.where(live_mask, jnp.exp(logit_values - row_max[:, :, None, None]), 0.0), axis=(2, 3)
    )
    slab_target = jnp.sum(jnp.where(target_mask, logit_values, 0.0), axis=(2, 3))
    row_total, target_score = lax.psum((local_total, slab_target), "item")
    losses = (row_max + jnp.log(row_total) - target_score).reshape(-1)
    own_rows = hidden.shape[0]
    row_loss = lax.dynamic_slice_in_dim(losses, owner_index * own_rows, own_rows)
    softmax_factor = coefficients(logit_values, live_mask, target_mask, row_max, row_total, weights)
    partial_value = jnp.einsum(
        "zmje,zjel->zml", softmax_factor, block_panels, preferred_element_type=jnp.float32
    ).reshape(-1, features)
    grad_hidden = lax.psum_scatter(partial_value, "item", scatter_dimension=0, tiled=True).astype(
        jnp.bfloat16
    )
    bucket_dispersal = spread_blocks(softmax_factor, slot_block, slot_valid, per_device)
    grad_table = lax.psum_scatter(
        jnp.einsum(
            "uszn,ush->hzn", bucket_dispersal, bucketed_rows, preferred_element_type=jnp.float32
        )
        .reshape(features // lax.axis_size("batch") * lax.axis_size("batch"), -1)
        .astype(jnp.bfloat16),
        "batch",
        scatter_dimension=0,
        tiled=True,
    )
    return (row_loss, grad_hidden, grad_table)


def solution(mesh):
    in_specs = (
        P(("batch", "item"), None),
        P("item", None),
        P("batch", None),
        P("batch"),
        P("batch"),
    )
    out_specs = (P(("batch", "item")), P(("batch", "item"), None), P("batch", "item"))
    return jax.shard_map(
        on_device, mesh=mesh, in_specs=in_specs, out_specs=out_specs, check_vma=False
    )
```

profile of v0, /device:TPU:6, one launch (start us, length us, event | category | flops | bytes accessed | tf_op | source)
XLA Modules:
  0.0 1205.4 jit_solution(16053970406659742117)
XLA Ops:
  7.2 0.7 fusion.19
  7.9 0.3 reduce_window_sum.11
  8.2 0.2 fusion.10
  8.4 0.2 select_reduce_fusion.1
  8.7 0.1 reshape.122
  8.7 208.2 %all_gather.3 = bf16[512,256]{1,0:T(8,128)(2,1)S(1)} all-gather(bf16[8,256]{1,0:T(8,128)(2,1)} %param.5), channel_id=1, replica_groups=mesh['batch'=8,'item'=64] {'item'}, dimensions={0}, use_global_device_ids=true | all-gather | bytes 266240 | tf_op jit(solution)/shard_map/all_gather | solution.py:71
  216.9 9.4 gather_fusion
  226.3 10.7 bitcast_reduce_fusion
  237.0 195.6 %pmax.7 = f32[8,64]{1,0:T(8,128)S(1)} all-reduce(f32[8,64]{1,0:T(8,128)S(1)} %get-tuple-element.12), channel_id=1, replica_groups=mesh['batch'=8,'item'=64] {'item'}, use_global_device_ids=true, to_apply=%region_4.5 | all-reduce | flops 512 | bytes 4096 | tf_op jit(solution)/shard_map/pmax | solution.py:81
  432.7 0.2 iota_compare_fusion
  433.0 0.1 broadcast_compare_fusion
  433.1 0.1 mul.19
  433.1 6.6 select_reduce_fusion
  439.8 205.7 %all-reduce = (f32[8,64]{1,0:T(8,128)S(1)}, f32[8,64]{1,0:T(8,128)S(1)}) all-reduce(f32[8,64]{1,0:T(8,128)S(1)} %get-tuple-element.4, f32[8,64]{1,0:T(8,128)S(1)} %get-tuple-element.3), channel_id=1, replica_groups=mesh['batch'=8,'item'=64] {'item'}, use_global_device_ids=true, to_apply=%region_8.9 | all-reduce | flops 1024 | bytes 8192 | tf_op jit(solution)/shard_map/psum | solution.py:86
  645.4 6.1 select_convert_fusion
  651.6 11.1 fusion.20
  662.7 0.2 reduce-scatter.5.cloned.1.call-start
  662.9 5.3 fusion.5
  668.3 18.1 %bitcast_convert_fusion = bf16[15,512,256]{2,1,0:T(8,128)(2,1)} fusion(bf16[8,64,256,1]{2,1,0,3:T(8,128)(2,1)S(1)} %bitcast.54, bf16[8,64,512,15]{2,3,1,0:T(8,128)(2,1)S(1)} %fusion.5), kind=kOutput, calls=%fused_computation.12 | convolution fusion | flops 2015232000 | bytes 12058624 | tf_op jit(solution)/shard_map/uszn,ush->hzn/dot_general | solution.py:99
  686.4 6.3 copy.9
  692.8 0.6 dynamic_slice.3
  693.4 417.3 %reduce-scatter.3.cloned.1.call-done = f32[8,256]{1,0:T(8,128)} async-done(((f32[512,256]{1,0:T(8,128)}), f32[8,256]{1,0:T(8,128)}) %reduce-scatter.3.cloned.1.call-update) | async-done | bytes 8208 | tf_op jit(solution)/shard_map/reduce_scatter | solution.py:94
  1110.7 1.3 convert_element_type.31
  1112.0 86.5 %reduce-scatter.5.cloned.1.call-done = bf16[32,7680]{1,0:T(8,128)(2,1)} async-done(((bf16[256,7680]{1,0:T(8,128)(2,1)}), bf16[32,7680]{1,0:T(8,128)(2,1)}) %reduce-scatter.5.cloned.1.call-update) | async-done | bytes 491536 | tf_op jit(solution)/shard_map/reduce_scatter | solution.py:98
  (16 shorter events, 0.3 us)
Async XLA Ops:
  7.2 1103.6 %reduce-scatter.3.cloned.1.call-start = ((), (), s32[]{:S(2)}) async-start(), calls=%async_computation.2 | async-start | bytes 532480 | tf_op jit(solution)/shard_map/reduce_scatter | solution.py:94
  226.3 206.4 %copy-start.1 = (s32[512]{0:T(512)S(1)}, s32[512]{0:T(512)}, u32[]{:S(2)}) copy-start(s32[512]{0:T(512)} %param.8) | copy-start | bytes 6148
  226.3 206.8 %copy-start.2 = (f32[512]{0:T(512)S(1)}, f32[512]{0:T(512)}, u32[]{:S(2)}) copy-start(f32[512]{0:T(512)} %param.9) | copy-start | bytes 6148
  651.6 11.1 copy-start
  662.7 535.9 %reduce-scatter.5.cloned.1.call-start = ((), (), s32[]{:S(2)}) async-start(), calls=%async_computation.3 | async-start | bytes 4423680 | tf_op jit(solution)/shard_map/reduce_scatter | solution.py:98
Sparse Core Ops, SparseCore 0:
  662.8 447.8 reduce-scatter.2
  1114.4 84.1 reduce-scatter.4
where the time goes:
time: 1210 us
  blocking collectives  609 us (50%)
  waiting for transfers between devices  504 us (42%)
  matrix products  45.2 us (4%)
  local copies, waits for them, and re-layouts  16.6 us (1%)
  other arithmetic  15.8 us (1%)
  between operations  14.1 us (1%)
    reduce_scatter x1, waiting for transfers between devices, on_device(): lax.psum_scatter(partial_value, 'item', scatter_dimension=0, tiled=True)  417 us
    all_gather x1, blocking collectives, on_device(): gathered = lax.all_gather(hidden, 'item', axis=0, tiled=True)  208 us
    psum x1, blocking collectives, on_device(): row_total, target_score = lax.psum((local_total, slab_target), 'item')  206 us
    pmax x1, blocking collectives, on_device(): row_max = lax.pmax(local_max, 'item')  196 us
    reduce_scatter x1, waiting for transfers between devices, on_device(): lax.psum_scatter(jnp.einsum('uszn,ush->hzn', bucket_dispersal, bucketed_r...  86.5 us
  transfers between devices with their start and end apart: 2, of which 2 were waited for; matrix products, arithmetic and copies ran while one was open for 3% of the time, Pallas kernels for 0%

commit v1 on v0

v1 whole, which is shorter than its diff:
```python
import functools

import jax
import jax.numpy as jnp
from jax import lax
from jax.experimental import pallas as pl
from jax.experimental.pallas import tpu as pltpu
from jax.sharding import PartitionSpec as P

MESH = pl.DeviceIdType.MESH
F32 = jnp.float32
BF16 = jnp.bfloat16

BLK = 512
NEGATIVE = -1e30
TILE = 256
LANES = 256
LAG_CORE = 2
LAG_CHIP = 5


def kernel(hid, meta, table, loss, gh_out, gt_out,
           tab, tab_t, hb, hf, ht, hp, metab, pbuf, mt, run, stx, stz, cbuf, ght, gs, gr, zs, zr,
           a_send, a_keep, a_recv, b_send, b_keep, b_recv, c_send,
           tsem, msem, zsem, xsem, sxsem, szsem, asem, bsem, csem, gxsem, gzsem):
    b = lax.axis_index("batch")
    i = lax.axis_index("item")
    zl, k = b // 2, b % 2
    par, half = zl % 2, zl // 2
    x, zh, y = i // 16, (i // 4) % 4, i % 4
    xy = x * 4 + y
    qm = half * 4 + zh
    n_half = tab.shape[0]
    n_tile = n_half // TILE
    rows = ht.shape[1]
    n_feat = tab.shape[1]
    share = rows // 2

    def z_dev(q):
        return ((par + 2 * (q // 4)) * 2 + k, x * 16 + (q % 4) * 4 + y)

    def xy_dev(v):
        return (b, (v // 4) * 16 + zh * 4 + v % 4)

    sibling = (zl * 2 + 1 - k, i)
    partner = ((zl + 1 - 2 * par) * 2 + k, i)
    other = ((par + 2 * (1 - half)) * 2 + k, i)

    def remote(src, dst, sems, j, dev):
        return pltpu.make_async_remote_copy(
            src_ref=src, dst_ref=dst, send_sem=sems.at[0, j], recv_sem=sems.at[1, j],
            device_id=dev, device_id_type=MESH)

    def loop(lo, hi, body):
        def step(j, carry):
            body(j)
            return carry
        lax.fori_loop(lo, hi, step, 0)

    table_copy = pltpu.make_async_copy(table.at[pl.ds(half * n_half, n_half), :], tab, tsem)
    table_copy.start()

    barrier = pltpu.get_barrier_semaphore()

    def greet(dev):
        pl.semaphore_signal(barrier, inc=1, device_id=dev, device_id_type=MESH)

    loop(1, 8, lambda j: greet(z_dev((qm + j) % 8)))
    loop(1, 16, lambda j: greet(xy_dev((xy + j) % 16)))
    greet(sibling)
    greet(partner)

    own = hid[...].astype(F32)
    hb[xy, qm] = jnp.concatenate([own[:, :128], own[:, 128:]], axis=0).astype(BF16)
    metab[half] = meta[...]
    pl.semaphore_wait(barrier, 24)

    loop(1, 8, lambda j: remote(hb.at[xy, qm], hb.at[xy, qm], zsem, j, z_dev((qm + j) % 8)).start())
    meta_copy = remote(metab.at[half], metab.at[half], msem, 0, other)
    meta_copy.start()

    def z_recv(j):
        q = (qm + 8 - j) % 8
        remote(hb.at[xy, q], hb.at[xy, q], zsem, j, z_dev(q)).wait_recv()

    loop(1, 8, z_recv)
    loop(1, 16, lambda j: remote(hb.at[xy], hb.at[xy], xsem, j, xy_dev((xy + j) % 16)).start())

    table_copy.wait()

    def flip_tile(t):
        tab_t[t] = tab[pl.ds(pl.multiple_of(t * TILE, TILE), TILE), :].astype(F32).T.astype(BF16)

    loop(0, n_tile, flip_tile)
    run[0:1, :] = jnp.full((1, rows), NEGATIVE, F32)
    run[1:3, :] = jnp.zeros((2, rows), F32)
    ght[...] = jnp.zeros(ght.shape, F32)

    def unpack(v):
        for q in range(8):
            piece = hb[v, q].astype(F32)
            n0 = (q // 4) * share + (v // 4) * 128 + (q % 4) * 32 + (v % 4) * 8
            n0 = pl.multiple_of(n0, 8)
            hf[pl.ds(n0, 8), 0:128] = piece[:8]
            hf[pl.ds(n0, 8), 128:256] = piece[8:]

    unpack(xy)

    def x_recv(j):
        v = (xy + 16 - j) % 16
        remote(hb.at[v], hb.at[v], xsem, j, xy_dev(v)).wait_recv()
        unpack(v)

    loop(1, 16, x_recv)
    for c in range(rows // 128):
        ht[:, c * 128:(c + 1) * 128] = hf[c * 128:(c + 1) * 128, :].T.astype(BF16)
    for rel in range(8):
        to = (par + (rel // 2) % 2) % 2 + 2 * ((half + rel % 2) % 2)
        f0 = pl.multiple_of((to * 2 + (k + rel // 4) % 2) * 32, 32)
        hp[rel * 32:(rel + 1) * 32, :] = ht[pl.ds(f0, 32), :]
    meta_copy.wait_send()
    remote(metab.at[1 - half], metab.at[1 - half], msem, 0, other).wait_recv()

    weight = jnp.concatenate([metab[0, 16:17, :], metab[1, 16:17, :]], axis=1)
    aim = jnp.concatenate([metab[0, 17:18, :], metab[1, 17:18, :]], axis=1) - (half * n_half).astype(F32)
    item_at = lax.broadcasted_iota(jnp.int32, (TILE, LANES), 0).astype(F32)

    def score_tile(t):
        items = tab[pl.ds(pl.multiple_of(t * TILE, TILE), TILE), :]
        block = (half * n_tile + t) * TILE // BLK
        bias = jnp.concatenate([metab[0, pl.ds(block, 1), :], metab[1, pl.ds(block, 1), :]], axis=1)
        here = aim - (t * TILE).astype(F32)
        for c in range(rows // LANES):
            at = slice(c * LANES, (c + 1) * LANES)
            s = jnp.dot(items, ht[:, at], preferred_element_type=F32) + bias[:, at]
            top = jnp.max(s, axis=0, keepdims=True)
            e = jnp.exp(s - top)
            pbuf[t, :, at] = e
            total = jnp.sum(e, axis=0, keepdims=True)
            hit = jnp.sum(jnp.where(item_at == here[:, at], s, 0.0), axis=0, keepdims=True)
            mt[t, :, at] = top
            old = run[0:1, at]
            new = jnp.maximum(old, top)
            run[0:1, at] = new
            run[1:2, at] = run[1:2, at] * jnp.exp(old - new) + total * jnp.exp(top - new)
            run[2:3, at] = run[2:3, at] + hit

    loop(0, n_tile, score_tile)

    for part in range(3):
        for c in range(8):
            stx[xy, part * 8 + c:part * 8 + c + 1, :] = run[part:part + 1, c * 128:(c + 1) * 128]
    loop(1, 16, lambda j: remote(stx.at[xy], stx.at[xy], sxsem, j, xy_dev((xy + j) % 16)).start())

    def sx_recv(j):
        v = (xy + 16 - j) % 16
        remote(stx.at[v], stx.at[v], sxsem, j, xy_dev(v)).wait_recv()

    def merge(ref, n):
        top = ref[0, 0:8, :]
        for v in range(1, n):
            top = jnp.maximum(top, ref[v, 0:8, :])
        total = jnp.zeros_like(top)
        hit = jnp.zeros_like(top)
        for v in range(n):
            total = total + ref[v, 8:16, :] * jnp.exp(ref[v, 0:8, :] - top)
            hit = hit + ref[v, 16:24, :]
        return top, total, hit

    loop(1, 16, sx_recv)
    top, total, hit = merge(stx, 16)
    stz[qm, 0:8, :] = top
    stz[qm, 8:16, :] = total
    stz[qm, 16:24, :] = hit
    loop(1, 8, lambda j: remote(stz.at[qm], stz.at[qm], szsem, j, z_dev((qm + j) % 8)).start())

    def sz_recv(j):
        q = (qm + 8 - j) % 8
        remote(stz.at[q], stz.at[q], szsem, j, z_dev(q)).wait_recv()

    loop(1, 8, sz_recv)
    top, total, hit = merge(stz, 8)
    loss[...] = top + jnp.log(total) - hit
    row_top = jnp.concatenate([top[c:c + 1, :] for c in range(8)], axis=1)
    row_total = jnp.concatenate([total[c:c + 1, :] for c in range(8)], axis=1)
    scale = weight / row_total

    def a_step(t):
        remote(a_recv.at[t], a_recv.at[t], asem, t, sibling).wait_recv()
        summed = a_keep[t] + a_recv[t].astype(F32)
        b_send[t] = summed[64:].astype(BF16)
        b_keep[t] = summed[:64]
        remote(b_send.at[t], b_recv.at[t], bsem, t, partner).start()

    def columns(which, t):
        return pl.ds(pl.multiple_of(which * n_half + t * TILE, TILE), TILE)

    def b_step(t):
        remote(b_recv.at[t], b_recv.at[t], bsem, t, partner).wait_recv()
        summed = (b_keep[t] + b_recv[t].astype(F32)).astype(BF16)
        c_send[t] = summed[32:]
        gt_out[:, columns(half, t)] = summed[:32]
        remote(c_send.at[t], gt_out.at[:, columns(half, t)], csem, t, other).start()

    def grad_tile(t):
        here = aim - (t * TILE).astype(F32)
        factor = jnp.exp(mt[t] - row_top) * scale
        for c in range(rows // LANES):
            at = slice(c * LANES, (c + 1) * LANES)
            coef = pbuf[t, :, at] * factor[:, at] - jnp.where(item_at == here[:, at], weight[:, at], 0.0)
            coef = coef.astype(BF16)
            cbuf[:, at] = coef
            ght[:, at] += jnp.dot(tab_t[t], coef, preferred_element_type=F32)
        g = lax.dot_general(hp[...], cbuf[...], (((1,), (1,)), ((), ())), preferred_element_type=F32)
        a_send[t] = g[128:].astype(BF16)
        a_keep[t] = g[:128]
        remote(a_send.at[t], a_recv.at[t], asem, t, sibling).start()

        @pl.when(t >= LAG_CORE)
        def _():
            a_step(t - LAG_CORE)

        @pl.when(t >= LAG_CHIP)
        def _():
            b_step(t - LAG_CHIP)

    loop(0, n_tile, grad_tile)

    for c in range(rows // 128):
        hf[c * 128:(c + 1) * 128, :] = ght[:, c * 128:(c + 1) * 128].T

    def gather_rows(v):
        pieces = []
        for q in range(8):
            n0 = pl.multiple_of((q // 4) * share + (v // 4) * 128 + (q % 4) * 32 + (v % 4) * 8, 8)
            pieces.append(hf[pl.ds(n0, 8), :])
        return jnp.concatenate(pieces, axis=0)

    def g_send(j):
        v = (xy + j) % 16
        gs[v] = gather_rows(v).astype(BF16)
        remote(gs.at[v], gr.at[xy], gxsem, j, xy_dev(v)).start()

    loop(1, 16, g_send)
    mine = gather_rows(xy)
    loop(n_tile - LAG_CORE, n_tile, a_step)

    def gx_recv(j, total):
        v = (xy + 16 - j) % 16
        remote(gr.at[v], gr.at[v], gxsem, j, xy_dev(v)).wait_recv()
        return total + gr[v].astype(F32)

    total = lax.fori_loop(1, 16, gx_recv, mine)
    for q in range(8):
        zs[q] = total[q * 8:(q + 1) * 8, :]
    loop(1, 8, lambda j: remote(zs.at[(qm + j) % 8], zr.at[qm], gzsem, j, z_dev((qm + j) % 8)).start())
    loop(n_tile - LAG_CHIP, n_tile, b_step)

    def gz_recv(j, total):
        q = (qm + 8 - j) % 8
        remote(zr.at[q], zr.at[q], gzsem, j, z_dev(q)).wait_recv()
        return total + zr[q]

    gh_out[...] = lax.fori_loop(1, 8, gz_recv, zs[qm]).astype(BF16)

    def z_sent(j):
        q = (qm + j) % 8
        remote(hb.at[xy, qm], hb.at[xy, qm], zsem, j, z_dev(q)).wait_send()
        remote(stz.at[qm], stz.at[qm], szsem, j, z_dev(q)).wait_send()
        remote(zs.at[q], zr.at[qm], gzsem, j, z_dev(q)).wait_send()

    def x_sent(j):
        v = (xy + j) % 16
        remote(hb.at[xy], hb.at[xy], xsem, j, xy_dev(v)).wait_send()
        remote(stx.at[xy], stx.at[xy], sxsem, j, xy_dev(v)).wait_send()
        remote(gs.at[v], gr.at[xy], gxsem, j, xy_dev(v)).wait_send()

    def t_sent(t):
        remote(a_send.at[t], a_recv.at[t], asem, t, sibling).wait_send()
        remote(b_send.at[t], b_recv.at[t], bsem, t, partner).wait_send()
        remote(c_send.at[t], gt_out.at[:, columns(half, t)], csem, t, other).wait_send()
        into = gt_out.at[:, columns(1 - half, t)]
        remote(c_send.at[t], into, csem, t, other).wait_recv()

    loop(1, 8, z_sent)
    loop(1, 16, x_sent)
    loop(0, n_tile, t_sent)


def on_device(hidden, item_table, bucket_blocks, targets, row_weight):
    i = lax.axis_index("item")
    half = lax.axis_index("batch") // 4
    items, feat = item_table.shape
    share = targets.shape[0]
    n_half = items // 2
    n_tile = n_half // TILE
    rows = 2 * share
    blocks = items // BLK
    local = bucket_blocks - i * blocks
    listed = jnp.any(local[None, :, :] == jnp.arange(16, dtype=jnp.int32)[:, None, None], axis=2)
    bias = jnp.where(listed, 0.0, NEGATIVE).astype(F32)
    bias = jnp.repeat(bias, share // bias.shape[1], axis=1)
    aim = (targets - i * items).astype(F32)
    meta = jnp.concatenate([bias, row_weight[None], aim[None], jnp.zeros((6, share), F32)], axis=0)

    vmem = pltpu.VMEM
    dma = pltpu.SemaphoreType.DMA
    scratch = [
        vmem((n_half, feat), BF16),
        vmem((n_tile, feat, TILE), BF16),
        vmem((16, 8, 16, 128), BF16),
        vmem((rows, feat), F32),
        vmem((feat, rows), BF16),
        vmem((feat, rows), BF16),
        vmem((2, 24, share), F32),
        vmem((n_tile, TILE, rows), F32),
        vmem((n_tile, 1, rows), F32),
        vmem((8, rows), F32),
        vmem((16, 24, 128), F32),
        vmem((8, 24, 128), F32),
        vmem((TILE, rows), BF16),
        vmem((feat, rows), F32),
        vmem((16, 64, feat), BF16),
        vmem((16, 64, feat), BF16),
        vmem((8, 8, feat), F32),
        vmem((8, 8, feat), F32),
        vmem((n_tile, 128, TILE), BF16),
        vmem((n_tile, 128, TILE), F32),
        vmem((n_tile, 128, TILE), BF16),
        vmem((n_tile, 64, TILE), BF16),
        vmem((n_tile, 64, TILE), F32),
        vmem((n_tile, 64, TILE), BF16),
        vmem((n_tile, 32, TILE), BF16),
        dma,
        dma((2, 1)),
        dma((2, 8)),
        dma((2, 16)),
        dma((2, 16)),
        dma((2, 8)),
        dma((2, n_tile)),
        dma((2, n_tile)),
        dma((2, n_tile)),
        dma((2, 16)),
        dma((2, 8)),
    ]
    in_vmem = pl.BlockSpec(memory_space=pltpu.VMEM)
    loss, gh, gt = pl.pallas_call(
        kernel,
        out_shape=(
            jax.ShapeDtypeStruct((8, 128), F32),
            jax.ShapeDtypeStruct(hidden.shape, BF16),
            jax.ShapeDtypeStruct((feat // 8, items), BF16),
        ),
        in_specs=[in_vmem, in_vmem, pl.BlockSpec(memory_space=pl.ANY)],
        out_specs=(in_vmem, in_vmem, in_vmem),
        scratch_shapes=scratch,
        compiler_params=pltpu.CompilerParams(
            collective_id=0, has_side_effects=True, vmem_limit_bytes=56 * 2**20),
    )(hidden, meta, item_table)
    own = lax.dynamic_slice_in_dim(loss.reshape(-1), half * share + i * hidden.shape[0], hidden.shape[0])
    return own, gh, gt


def solution(mesh):
    in_specs = (
        P(("batch", "item"), None),
        P("item", None),
        P("batch", None),
        P("batch"),
        P("batch"),
    )
    out_specs = (P(("batch", "item")), P(("batch", "item"), None), P("batch", "item"))
    return jax.shard_map(on_device, mesh=mesh, in_specs=in_specs, out_specs=out_specs, check_vma=False)
```

time: 1210 us -> 94.8 us (0.08)
  blocking collectives: 609 us -> 0 us
  waiting for transfers between devices: 504 us -> 0 us
  Pallas kernels: 0 us -> 86.1 us
  matrix products: 45.2 us -> 0 us
  between operations: 14.1 us -> 0.68 us
  other arithmetic: 15.8 us -> 3.11 us
    reduce_scatter x2 -> x0, waiting for transfers between devices: 504 us -> none  [the longest x1 417 us: on_device(): lax.psum_scatter(partial_value, 'item', scatter_dimension=0, tiled=True)]
    all_gather x1 -> x0, blocking collectives: 208 us -> none  [on_device(): gathered = lax.all_gather(hidden, 'item', axis=0, tiled=True)]
    psum x1 -> x0, blocking collectives: 206 us -> none  [on_device(): row_total, target_score = lax.psum((local_total, slab_target), 'item')]
    pmax x1 -> x0, blocking collectives: 196 us -> none  [on_device(): row_max = lax.pmax(local_max, 'item')]
    pallas_call x0 -> x1, Pallas kernels: none -> 86.1 us  [on_device(): pl.pallas_call(kernel, out_shape=(jax.ShapeDtypeStruct((8, 128), F32), ja...]
    dot_general x4 -> x0, matrix products: 45.2 us -> none  [the longest x1 18.1 us: on_device(): jnp.einsum('uszn,ush->hzn', bucket_dispersal, bucketed_rows, preferred_el...]
  transfers between devices with their start and end apart: 2 -> 0, of which waited for: 2 -> 0; matrix products, arithmetic and copies ran while one was open for 3% -> 0% of each run, Pallas kernels for 0% -> 0%
where the time goes in v1:
time: 94.8 us; the launch traced here: 94.5 us
  Pallas kernels  86.1 us (91%)
  local copies, waits for them, and re-layouts  4.62 us (5%)
  other arithmetic  3.11 us (3%)
    pallas_call x1, Pallas kernels, on_device(): pl.pallas_call(kernel, out_shape=(jax.ShapeDtypeStruct((8, 128), F32), ja...  86.1 us
    unnamed x2, local copies, waits for them, and re-layouts  3.11 us

profile of v1, /device:TPU:6, one launch (start us, length us, event | category | flops | bytes accessed | tf_op | source)
XLA Modules:
  0.0 94.5 jit_solution(16618074051649054673)
XLA Ops:
  0.7 0.1 pad.3.clone
  0.7 0.7 subtract_convert_fusion
  1.4 0.7 broadcast_subtract_fusion
  2.1 0.4 fusion
  2.5 0.1 broadcast_in_dim.24
  2.6 0.1 reshape.13
  2.6 1.4 %maximum_maximum_fusion.meta = f32[24,512]{1,0:T(8,128)} fusion(f32[1,512]{1,0:T(1,128)S(1)} %bitcast.3, f32[1,512]{1,0:T(1,128)} %bitcast.4, f32[16,512]{1,0:T(8,128)S(1)} %reshape.13, f32[24]{0:T(128)S(1)} %pad.3.clone), kind=kLoop, calls=%fused_computation.2 | loop fusion | flops 36864 | bytes 86112 | tf_op jit(solution)/shard_map/concatenate | solution.py:304
  4.0 86.1 %shard_map.76 = (f32[8,128]{1,0:T(8,128)}, bf16[8,256]{1,0:T(8,128)(2,1)}, bf16[32,7680]{1,0:T(8,128)(2,1)}) custom-call(bf16[8,256]{1,0:T(8,128)(2,1)} %hid.1, f32[24,512]{1,0:T(8,128)} %maximum_maximum_fusion.meta, bf16[7680,256]{1,0:T(8,128)(2,1)} %table.1), custom_call_target="tpu_custom_call" | custom-call | tf_op jit(solution)/shard_map/pallas_call | solution.py:347
  90.1 1.3 %dynamic_slice.3 = f32[8]{0:T(128)} dynamic-slice(f32[1024]{0:T(1024)} %bitcast.5, s32[]{:T(128)S(6)} %select_n.14), dynamic_slice_sizes={8} | dynamic-slice | bytes 68 | tf_op jit(solution)/shard_map/dynamic_slice | solution.py:360
  91.4 1.3 %copy.10 = bf16[8,256]{1,0:T(8,128)(2,1)} copy(bf16[8,256]{1,0:T(8,128)(2,1)} %get-tuple-element.13) | data formatting | bytes 8192
  92.6 1.8 %copy.11 = bf16[32,7680]{1,0:T(8,128)(2,1)} copy(bf16[32,7680]{1,0:T(8,128)(2,1)} %get-tuple-element.14) | data formatting | bytes 983040
  (2 shorter events, 0.0 us)

commit v2 on v1

v2 whole, which is shorter than its diff:
```python
import jax
import jax.numpy as jnp
from jax import lax
from jax.experimental import pallas as pl
from jax.experimental.pallas import tpu as pltpu
from jax.sharding import PartitionSpec as P

MESH = pl.DeviceIdType.MESH
F32 = jnp.float32
BF16 = jnp.bfloat16

BLK = 512
NEGATIVE = -1e30
TILE = 256
GROUP = 3
LAG_CORE = 2
LAG_CHIP = 5
EARLY = 2
REACH = (0, 1, 7, 2, 6, 3, 5, 4)
PIECES = ((0, 1), (1, 3), (3, 5), (5, 7), (7, 8))


def kernel(hid_hbm, lists_hbm, targets_hbm, weights_hbm, table, loss, gh_out, gt_out,
           hid, lists, targets, weights, tab, tab_t, hb, hf, ht, hp, metab, bias, pbuf, mt, stx, stz, cbuf, obuf, ut, vt, gs, gr, zs, zr,
           a_send, a_keep, a_recv, b_send, b_keep, b_recv, c_send,
           tsem, insem, msem, zsem, xsem, sxsem, szsem, hxsem, hzsem, asem, bsem, csem, gxsem, gzsem):
    b = lax.axis_index("batch")
    i = lax.axis_index("item")
    zl, k = b // 2, b % 2
    par, half = zl % 2, zl // 2
    x, zh, y = i // 16, (i // 4) % 4, i % 4
    xy = x * 4 + y
    qm = zh * 2 + half
    n_half = tab.shape[0]
    n_tile = n_half // TILE
    n_group = n_tile // GROUP

    def z_dev(q):
        return ((par + 2 * (q % 2)) * 2 + k, x * 16 + (q // 2) * 4 + y)

    def xy_dev(v):
        return (b, (v // 4) * 16 + zh * 4 + v % 4)

    sibling = (zl * 2 + 1 - k, i)
    partner = ((zl + 1 - 2 * par) * 2 + k, i)
    other = ((par + 2 * (1 - half)) * 2 + k, i)

    def remote(src, dst, sems, j, dev):
        return pltpu.make_async_remote_copy(
            src_ref=src, dst_ref=dst, send_sem=sems.at[0, j], recv_sem=sems.at[1, j],
            device_id=dev, device_id_type=MESH)

    def loop(lo, hi, body):
        def step(j, carry):
            body(j)
            return carry
        lax.fori_loop(lo, hi, step, 0)

    table_copy = pltpu.make_async_copy(table.at[pl.ds(half * n_half, n_half), :], tab, tsem)
    table_copy.start()
    inputs = [
        pltpu.make_async_copy(src, dst, insem.at[n])
        for n, (src, dst) in enumerate(
            ((hid_hbm, hid), (lists_hbm, lists), (targets_hbm, targets), (weights_hbm, weights)))
    ]
    for copy in inputs:
        copy.start()

    barrier = pltpu.get_barrier_semaphore()

    def greet(dev):
        pl.semaphore_signal(barrier, inc=1, device_id=dev, device_id_type=MESH)

    for j in (4, 3, 5, 2, 6, 1, 7):
        greet(z_dev((qm + j) % 8))
    loop(1, 16, lambda j: greet(xy_dev((xy + j) % 16)))
    greet(sibling)
    greet(partner)

    for copy in inputs:
        copy.wait()
    own = hid[...].astype(F32)
    hb[xy, 0] = jnp.concatenate([own[:, :128], own[:, 128:]], axis=0).astype(BF16)
    metab[half, 0:8, :] = lists[...].astype(F32)
    lane = lax.broadcasted_iota(jnp.int32, (1, 128), 1)
    for at, ref in ((8, targets), (12, weights)):
        rows = ref[...].astype(F32)
        turned = [rows if d == 0 else pltpu.roll(rows, 32 * d, 1) for d in range(4)]
        for to in range(4):
            line = jnp.zeros((1, 128), F32)
            for fx in range(4):
                line = jnp.where(lane // 32 == fx, turned[(fx - to) % 4][fx:fx + 1, :], line)
            metab[half, at + to:at + to + 1, :] = line
    pl.semaphore_wait(barrier, 24)

    for j in (4, 3, 5, 2, 6, 1, 7):
        remote(hb.at[xy, 0], hb.at[xy, REACH.index(8 - j)], zsem, 8 - j, z_dev((qm + j) % 8)).start()
    meta_copy = remote(metab.at[half], metab.at[half], msem, 0, other)
    meta_copy.start()

    def x_copy(piece, v_from, v_to, j):
        lo, hi = PIECES[piece]
        ref = hb.at[v_from, lo:hi]
        return remote(ref, ref, xsem, piece * 16 + j, xy_dev(v_to))

    def x_send(piece):
        loop(1, 16, lambda j: x_copy(piece, xy, (xy + j) % 16, j).start())

    def z_recv(piece):
        for s in range(*PIECES[piece]):
            q = (qm + REACH[s]) % 8
            remote(hb.at[xy, s], hb.at[xy, s], zsem, REACH[s], z_dev(q)).wait_recv()

    x_send(0)
    table_copy.wait()

    def flip_group(g):
        part = tab[pl.ds(pl.multiple_of(g * GROUP * TILE, TILE), GROUP * TILE), :]
        tab_t[g] = part.astype(F32).T.astype(BF16)

    loop(0, 1, flip_group)
    z_recv(1)
    x_send(1)
    loop(1, 2, flip_group)
    z_recv(2)
    x_send(2)
    loop(2, 3, flip_group)

    meta_copy.wait_send()
    remote(metab.at[1 - half], metab.at[1 - half], msem, 0, other).wait_recv()
    base = (i * 2 * n_half // BLK + half * (n_tile * TILE // BLK)).astype(F32)
    bucket = lax.broadcasted_iota(jnp.int32, (8, 128), 0)
    column = lax.broadcasted_iota(jnp.int32, (8, 128), 1) // 32
    for g in range(2):
        local = metab[g, 0:8, :] - base
        for blk in range(8):
            listed = jnp.max(jnp.where(local == blk, 1.0, 0.0), axis=1, keepdims=True)
            for side in range(2):
                spread = jnp.where(bucket == column * 2 + side, listed, 0.0)
                line = jnp.max(spread, axis=0, keepdims=True)
                bias[g * 2 + side, blk:blk + 1, :] = jnp.where(line > 0.0, 0.0, NEGATIVE)

    aim_base = (i * 2 * n_half + half * n_half).astype(F32)
    aims, weight = [], []
    for q in range(8):
        aims.append(metab[q % 2, 8 + q // 2:9 + q // 2, :] - aim_base)
        weight.append(metab[q % 2, 12 + q // 2:13 + q // 2, :])
    aim = jnp.concatenate(aims, axis=0)
    weight = jnp.concatenate(weight, axis=0)
    item_at = lax.broadcasted_iota(jnp.int32, (TILE, 128), 0).astype(F32)

    def unpack(piece, v):
        for s in range(*PIECES[piece]):
            part = hb[v, s].astype(F32)
            rows = pl.ds(pl.multiple_of(v * 8, 8), 8)
            hf[s, rows, 0:128] = part[:8]
            hf[s, rows, 128:256] = part[8:]

    def score(piece):
        def x_recv(j):
            v = (xy + 16 - j) % 16
            x_copy(piece, v, v, j).wait_recv()
            unpack(piece, v)

        unpack(piece, xy)
        loop(1, 16, x_recv)
        places = []
        for s in range(*PIECES[piece]):
            q = (qm + REACH[s]) % 8
            ht[q] = hf[s].T.astype(BF16)
            q_aim = metab[q % 2, pl.ds(8 + q // 2, 1), :] - aim_base
            places.append((q, (q % 2) * 2 + q // 4, q_aim))

        def score_group(g, carry):
            carry = list(carry)
            for u in range(GROUP):
                t = g * GROUP + u
                items = tab[pl.ds(pl.multiple_of(t * TILE, TILE), TILE), :]
                for at, (q, side, q_aim) in enumerate(places):
                    old, total, hit = carry[at]
                    s = jnp.dot(items, ht[q], preferred_element_type=F32)
                    top = jnp.max(s, axis=0, keepdims=True)
                    e = jnp.exp(s - top)
                    pbuf[q, t] = e
                    top = top + bias[side, pl.ds((t + half) // 2, 1), :]
                    mt[t, pl.ds(q, 1), :] = top
                    new = jnp.maximum(old, top)
                    total = total * jnp.exp(old - new) + jnp.sum(e, axis=0, keepdims=True) * jnp.exp(top - new)
                    here = q_aim - (t * TILE).astype(F32)
                    hit = hit + jnp.sum(jnp.where(item_at == here, s, 0.0), axis=0, keepdims=True)
                    carry[at] = (new, total, hit)
            return tuple(carry)

        zero = jnp.zeros((1, 128), F32)
        done = lax.fori_loop(0, n_group, score_group, tuple((zero + NEGATIVE, zero, zero) for _ in places))
        for (q, _, _), (top, total, hit) in zip(places, done):
            stx[xy, pl.ds(q, 1), :] = top
            stx[xy, pl.ds(8 + q, 1), :] = total
            stx[xy, pl.ds(16 + q, 1), :] = hit

    score(0)
    z_recv(3)
    x_send(3)
    z_recv(4)
    x_send(4)
    loop(3, n_group, flip_group)
    for piece in range(1, 5):
        score(piece)

    def sx_copy(hits, j, v_from, v_to):
        ref = stx.at[v_from, 16:24] if hits else stx.at[v_from, 0:16]
        return remote(ref, ref, hxsem if hits else sxsem, j, xy_dev(v_to))

    def sz_copy(hits, j, q_from, q_to):
        ref = stz.at[q_from, 16:24] if hits else stz.at[q_from, 0:16]
        return remote(ref, ref, hzsem if hits else szsem, j, z_dev(q_to))

    loop(1, 16, lambda j: sx_copy(False, j, xy, (xy + j) % 16).start())
    loop(1, 16, lambda j: sx_copy(True, j, xy, (xy + j) % 16).start())
    top_here = stx[xy, 0:8, :]
    hit_here = stx[xy, 16:24, :]

    for rel in range(8):
        to = (par + (rel // 2) % 2) % 2 + 2 * ((half + rel % 2) % 2)
        f0 = pl.multiple_of((to * 2 + (k + rel // 4) % 2) * 32, 32)
        for q in range(8):
            hp[rel * 32:(rel + 1) * 32, q * 128:(q + 1) * 128] = ht[q, pl.ds(f0, 32), :]

    ut[...] = jnp.zeros(ut.shape, F32)
    vt[...] = jnp.zeros(vt.shape, F32)

    def early_group(g):
        for u in range(GROUP):
            t = g * GROUP + u
            here = aim - (t * TILE).astype(F32)
            factor = jnp.exp(mt[t] - top_here)
            for q in range(8):
                at = slice(q * 128, (q + 1) * 128)
                aimed = item_at == here[q:q + 1, :]
                cbuf[u * TILE:(u + 1) * TILE, at] = jnp.where(aimed, 0.0, pbuf[q, t] * factor[q:q + 1, :]).astype(BF16)
                obuf[u * TILE:(u + 1) * TILE, at] = jnp.where(aimed, 1.0, 0.0).astype(BF16)
        ut[...] += jnp.dot(tab_t[g], cbuf[...], preferred_element_type=F32)
        vt[...] += jnp.dot(tab_t[g], obuf[...], preferred_element_type=F32)

    loop(0, EARLY, early_group)

    def merge(ref, n):
        top = ref[0, 0:8, :]
        for v in range(1, n):
            top = jnp.maximum(top, ref[v, 0:8, :])
        total = jnp.zeros_like(top)
        for v in range(n):
            total = total + ref[v, 8:16, :] * jnp.exp(ref[v, 0:8, :] - top)
        return top, total

    def sum_hits(ref, n):
        hit = ref[0, 16:24, :]
        for v in range(1, n):
            hit = hit + ref[v, 16:24, :]
        return hit

    def sx_wait(hits):
        def wait(j):
            v = (xy + 16 - j) % 16
            sx_copy(hits, j, v, v).wait_recv()
        loop(1, 16, wait)

    def sz_wait(hits):
        for j in range(1, 8):
            q = (qm + 8 - j) % 8
            sz_copy(hits, j, q, q).wait_recv()

    sx_wait(False)
    top, total = merge(stx, 16)
    stz[qm, 0:8, :] = top
    stz[qm, 8:16, :] = total
    for j in (4, 3, 5, 2, 6, 1, 7):
        sz_copy(False, j, qm, (qm + j) % 8).start()
    sx_wait(True)
    stz[qm, 16:24, :] = sum_hits(stx, 16)
    for j in (4, 3, 5, 2, 6, 1, 7):
        sz_copy(True, j, qm, (qm + j) % 8).start()
    loop(EARLY, n_group, early_group)
    sz_wait(False)
    top, total = merge(stz, 8)
    scale = weight / total

    def a_step(t):
        remote(a_recv.at[t], a_recv.at[t], asem, t, sibling).wait_recv()
        summed = a_keep[t] + a_recv[t].astype(F32)
        b_send[t] = summed[64:].astype(BF16)
        b_keep[t] = summed[:64]
        remote(b_send.at[t], b_recv.at[t], bsem, t, partner).start()

    def columns(which, t):
        return pl.ds(pl.multiple_of(which * n_half + t * TILE, TILE), TILE)

    def b_step(t):
        remote(b_recv.at[t], b_recv.at[t], bsem, t, partner).wait_recv()
        summed = (b_keep[t] + b_recv[t].astype(F32)).astype(BF16)
        c_send[t] = summed[32:]
        gt_out[:, columns(half, t)] = summed[:32]
        remote(c_send.at[t], gt_out.at[:, columns(half, t)], csem, t, other).start()

    def grad_tile(t):
        here = aim - (t * TILE).astype(F32)
        factor = jnp.exp(mt[t] - top) * scale
        for q in range(8):
            at = slice(q * 128, (q + 1) * 128)
            less = jnp.where(item_at == here[q:q + 1, :], weight[q:q + 1, :], 0.0)
            cbuf[0:TILE, at] = (pbuf[q, t] * factor[q:q + 1, :] - less).astype(BF16)
        g = lax.dot_general(hp[...], cbuf[0:TILE, :], (((1,), (1,)), ((), ())), preferred_element_type=F32)
        a_send[t] = g[128:].astype(BF16)
        a_keep[t] = g[:128]
        remote(a_send.at[t], a_recv.at[t], asem, t, sibling).start()

        @pl.when(t >= LAG_CORE)
        def _():
            a_step(t - LAG_CORE)

        @pl.when(t >= LAG_CHIP)
        def _():
            b_step(t - LAG_CHIP)

    loop(0, LAG_CORE, grad_tile)

    on_here = (aim >= 0.0) & (aim < float(n_half))
    chance = jnp.exp(jnp.where(on_here, hit_here, NEGATIVE) - top) / total
    of_target = weight * (chance - 1.0)
    of_rest = jnp.exp(top_here - top) * scale
    for q in range(8):
        at = slice(q * 128, (q + 1) * 128)
        grad = ut[:, at] * of_rest[q:q + 1, :] + vt[:, at] * of_target[q:q + 1, :]
        hf[q] = grad.T

    def gather_rows(v):
        rows = pl.ds(pl.multiple_of(v * 8, 8), 8)
        return jnp.concatenate([hf[q, rows, :] for q in range(8)], axis=0)

    def g_send(j):
        v = (xy + j) % 16
        gs[v] = gather_rows(v).astype(BF16)
        remote(gs.at[v], gr.at[xy], gxsem, j, xy_dev(v)).start()

    loop(1, 16, g_send)
    mine = gather_rows(xy)
    loop(LAG_CORE, n_tile, grad_tile)
    loop(n_tile - LAG_CORE, n_tile, a_step)

    def gx_recv(j, total):
        v = (xy + 16 - j) % 16
        remote(gr.at[v], gr.at[v], gxsem, j, xy_dev(v)).wait_recv()
        return total + gr[v].astype(F32)

    summed = lax.fori_loop(1, 16, gx_recv, mine)
    for q in range(8):
        zs[q] = summed[q * 8:(q + 1) * 8, :]
    for j in (4, 3, 5, 2, 6, 1, 7):
        remote(zs.at[(qm + j) % 8], zr.at[qm], gzsem, j, z_dev((qm + j) % 8)).start()
    loop(n_tile - LAG_CHIP, n_tile, b_step)

    sz_wait(True)
    loss_all = top + jnp.log(total) - sum_hits(stz, 8)
    bucket_is_own = bucket == qm
    line = jnp.sum(jnp.where(bucket_is_own, loss_all, 0.0), axis=0, keepdims=True)
    loss[...] = pltpu.roll(jnp.broadcast_to(line, (8, 128)), (128 - xy * 8) % 128, 1)

    grad = zs[qm]
    for j in range(1, 8):
        q = (qm + 8 - j) % 8
        remote(zr.at[q], zr.at[q], gzsem, j, z_dev(q)).wait_recv()
        grad = grad + zr[q]
    gh_out[...] = grad.astype(BF16)

    for j in range(1, 8):
        q = (qm + j) % 8
        remote(hb.at[xy, 0], hb.at[xy, REACH.index(8 - j)], zsem, 8 - j, z_dev(q)).wait_send()
        sz_copy(False, j, qm, q).wait_send()
        sz_copy(True, j, qm, q).wait_send()
        remote(zs.at[q], zr.at[qm], gzsem, j, z_dev(q)).wait_send()

    def x_sent(j):
        v = (xy + j) % 16
        for piece in range(5):
            x_copy(piece, xy, v, j).wait_send()
        sx_copy(False, j, xy, v).wait_send()
        sx_copy(True, j, xy, v).wait_send()
        remote(gs.at[v], gr.at[xy], gxsem, j, xy_dev(v)).wait_send()

    def t_sent(t):
        remote(a_send.at[t], a_recv.at[t], asem, t, sibling).wait_send()
        remote(b_send.at[t], b_recv.at[t], bsem, t, partner).wait_send()
        remote(c_send.at[t], gt_out.at[:, columns(half, t)], csem, t, other).wait_send()
        into = gt_out.at[:, columns(1 - half, t)]
        remote(c_send.at[t], into, csem, t, other).wait_recv()

    loop(1, 16, x_sent)
    loop(0, n_tile, t_sent)


def finish(loss, gh, gt, loss_out, gh_out, gt_out, sem):
    copies = [pltpu.make_async_copy(gt, gt_out, sem.at[0]), pltpu.make_async_copy(gh, gh_out, sem.at[1])]
    for c in copies:
        c.start()
    for r in range(loss_out.shape[0]):
        loss_out[r] = loss[0, r]
    for c in copies:
        c.wait()


def on_device(hidden, item_table, bucket_blocks, targets, row_weight):
    items, feat = item_table.shape
    n_half = items // 2
    n_tile = n_half // TILE
    n_group = n_tile // GROUP
    rows = 8 * 128

    vmem = pltpu.VMEM
    dma = pltpu.SemaphoreType.DMA
    scratch = [
        vmem(hidden.shape, BF16),
        vmem(bucket_blocks.shape, jnp.int32),
        vmem((4, 128), jnp.int32),
        vmem((4, 128), F32),
        vmem((n_half, feat), BF16),
        vmem((n_group, feat, GROUP * TILE), BF16),
        vmem((16, 8, 16, 128), BF16),
        vmem((8, 128, feat), F32),
        vmem((8, feat, 128), BF16),
        vmem((feat, rows), BF16),
        vmem((2, 16, 128), F32),
        vmem((4, 8, 128), F32),
        vmem((8, n_tile, TILE, 128), F32),
        vmem((n_tile, 8, 128), F32),
        vmem((16, 24, 128), F32),
        vmem((8, 24, 128), F32),
        vmem((GROUP * TILE, rows), BF16),
        vmem((GROUP * TILE, rows), BF16),
        vmem((feat, rows), F32),
        vmem((feat, rows), F32),
        vmem((16, 64, feat), BF16),
        vmem((16, 64, feat), BF16),
        vmem((8, 8, feat), F32),
        vmem((8, 8, feat), F32),
        vmem((n_tile, 128, TILE), BF16),
        vmem((n_tile, 128, TILE), F32),
        vmem((n_tile, 128, TILE), BF16),
        vmem((n_tile, 64, TILE), BF16),
        vmem((n_tile, 64, TILE), F32),
        vmem((n_tile, 64, TILE), BF16),
        vmem((n_tile, 32, TILE), BF16),
        dma,
        dma((4,)),
        dma((2, 1)),
        dma((2, 8)),
        dma((2, 80)),
        dma((2, 16)),
        dma((2, 8)),
        dma((2, 16)),
        dma((2, 8)),
        dma((2, n_tile)),
        dma((2, n_tile)),
        dma((2, n_tile)),
        dma((2, 16)),
        dma((2, 8)),
    ]
    in_vmem = pl.BlockSpec(memory_space=pltpu.VMEM)
    in_smem = pl.BlockSpec(memory_space=pltpu.SMEM)
    anywhere = pl.BlockSpec(memory_space=pl.ANY)
    gh_shape = jax.ShapeDtypeStruct(hidden.shape, BF16)
    gt_shape = jax.ShapeDtypeStruct((feat // 8, items), BF16)
    loss, gh, gt = pl.pallas_call(
        kernel,
        out_shape=(jax.ShapeDtypeStruct((8, 128), F32), gh_shape, gt_shape),
        in_specs=[pl.BlockSpec(memory_space=pltpu.HBM)] * 5,
        out_specs=(in_vmem, in_vmem, in_vmem),
        scratch_shapes=scratch,
        compiler_params=pltpu.CompilerParams(
            collective_id=0, has_side_effects=True, vmem_limit_bytes=56 * 2**20),
    )(hidden, bucket_blocks, targets.reshape(4, 128), row_weight.reshape(4, 128), item_table)
    return pl.pallas_call(
        finish,
        out_shape=(jax.ShapeDtypeStruct((hidden.shape[0],), F32), gh_shape, gt_shape),
        in_specs=[in_smem, in_vmem, in_vmem],
        out_specs=(in_smem, anywhere, anywhere),
        scratch_shapes=[dma((2,))],
    )(loss, gh, gt)


def solution(mesh):
    in_specs = (
        P(("batch", "item"), None),
        P("item", None),
        P("batch", None),
        P("batch"),
        P("batch"),
    )
    out_specs = (P(("batch", "item")), P(("batch", "item"), None), P("batch", "item"))
    return jax.shard_map(on_device, mesh=mesh, in_specs=in_specs, out_specs=out_specs, check_vma=False)
```

time: 94.8 us -> 80.4 us (0.85); the launches traced: 94.5 us -> 79 us
  Pallas kernels: 86.1 us -> 78.3 us
  local copies, waits for them, and re-layouts: 4.62 us -> 0 us
  other arithmetic: 3.11 us -> 0 us
    pallas_call x1 -> x2, Pallas kernels: 86.1 us -> 78.3 us  [the longest x1 76 us: on_device(): pl.pallas_call(kernel, out_shape=(jax.ShapeDtypeStruct((8, 128), F32), gh...]
    unnamed x2 -> x0, local copies, waits for them, and re-layouts: 3.11 us -> none
    concatenate x1 -> x0, other arithmetic: 1.38 us -> none  [on_device(): jnp.concatenate([bias, row_weight[None], aim[None], jnp.zeros((6, share),...]
    dynamic_slice x1 -> x0, local copies, waits for them, and re-layouts: 1.27 us -> none  [on_device(): lax.dynamic_slice_in_dim(loss.reshape(-1), half * share + i * hidden.shap...]
where the time goes in v2:
time: 80.4 us; the launch traced here: 79 us
  Pallas kernels  78.3 us (97%)
    pallas_call x1, Pallas kernels, on_device(): pl.pallas_call(kernel, out_shape=(jax.ShapeDtypeStruct((8, 128), F32), gh...  76 us
    pallas_call x1, Pallas kernels, on_device(): pl.pallas_call(finish, out_shape=(jax.ShapeDtypeStruct((hidden.shape[0],)...  2.36 us

profile of v2, /device:TPU:6, one launch (start us, length us, event | category | flops | bytes accessed | tf_op | source)
XLA Modules:
  0.0 79.0 jit_solution(2293019150350436577)
XLA Ops:
  0.6 76.0 %shard_map.76 = (f32[8,128]{1,0:T(8,128)}, bf16[8,256]{1,0:T(8,128)(2,1)}, bf16[32,7680]{1,0:T(8,128)(2,1)}) custom-call(bf16[8,256]{1,0:T(8,128)(2,1)} %hid_hbm.1, s32[8,128]{1,0:T(8,128)} %lists_hbm.1, s32[4,128]{1,0:T(4,128)} %bitcast.2, f32[4,128]{1,0:T(4,128)} %bitcast.3, bf16[7680,256]{1,0:T(8,128)(2,1)} %table.1), custom_call_target="tpu_custom_call" | custom-call | tf_op jit(solution)/shard_map/pallas_call | solution.py:472
  76.6 2.4 %shard_map.77 = (f32[8]{0:T(128)}, bf16[8,256]{1,0:T(8,128)(2,1)}, bf16[32,7680]{1,0:T(8,128)(2,1)}) custom-call(f32[8,128]{1,0:T(8,128)} %get-tuple-element.6.loss, bf16[8,256]{1,0:T(8,128)(2,1)} %get-tuple-element.7.gh, bf16[32,7680]{1,0:T(8,128)(2,1)} %get-tuple-element.8.gt), custom_call_target="tpu_custom_call" | custom-call | tf_op jit(solution)/shard_map/pallas_call | solution.py:481

commit v3 on v2

--- a/solution.py
+++ b/solution.py
@@ -1,3 +1,5 @@
+import functools
+
 import jax
 import jax.numpy as jnp
 from jax import lax
@@ -13,15 +15,16 @@
 NEGATIVE = -1e30
 TILE = 256
 GROUP = 3
-LAG_CORE = 2
-LAG_CHIP = 5
+LAG_CORE = 4
+LAG_CHIP = 9
+HIDDEN_AT = 2
 EARLY = 2
 REACH = (0, 1, 7, 2, 6, 3, 5, 4)
-PIECES = ((0, 1), (1, 3), (3, 5), (5, 7), (7, 8))
+PIECES = ((0, 3), (3, 5), (5, 8))
 
 
 def kernel(hid_hbm, lists_hbm, targets_hbm, weights_hbm, table, loss, gh_out, gt_out,
-           hid, lists, targets, weights, tab, tab_t, hb, hf, ht, hp, metab, bias, pbuf, mt, stx, stz, cbuf, obuf, ut, vt, gs, gr, zs, zr,
+           hid, lists, targets, weights, tab, tab_t, hb, hf, ht, hw, hp, metab, bias, pbuf, mt, stx, stz, cbuf, obuf, ut, vt, gs, gr, zs, zk, zr,
            a_send, a_keep, a_recv, b_send, b_keep, b_recv, c_send,
            tsem, insem, msem, zsem, xsem, sxsem, szsem, hxsem, hzsem, asem, bsem, csem, gxsem, gzsem):
     b = lax.axis_index("batch")
@@ -91,6 +94,13 @@
             for fx in range(4):
                 line = jnp.where(lane // 32 == fx, turned[(fx - to) % 4][fx:fx + 1, :], line)
             metab[half, at + to:at + to + 1, :] = line
+    table_copy.wait()
+
+    def flip_group(g):
+        part = tab[pl.ds(pl.multiple_of(g * GROUP * TILE, TILE), GROUP * TILE), :]
+        tab_t[g] = part.astype(F32).T.astype(BF16)
+
+    loop(0, n_group, flip_group)
     pl.semaphore_wait(barrier, 24)
 
     for j in (4, 3, 5, 2, 6, 1, 7):
@@ -108,23 +118,12 @@
 
     def z_recv(piece):
         for s in range(*PIECES[piece]):
-            q = (qm + REACH[s]) % 8
-            remote(hb.at[xy, s], hb.at[xy, s], zsem, REACH[s], z_dev(q)).wait_recv()
-
+            if s > 0:
+                q = (qm + REACH[s]) % 8
+                remote(hb.at[xy, s], hb.at[xy, s], zsem, REACH[s], z_dev(q)).wait_recv()
+
+    z_recv(0)
     x_send(0)
-    table_copy.wait()
-
-    def flip_group(g):
-        part = tab[pl.ds(pl.multiple_of(g * GROUP * TILE, TILE), GROUP * TILE), :]
-        tab_t[g] = part.astype(F32).T.astype(BF16)
-
-    loop(0, 1, flip_group)
-    z_recv(1)
-    x_send(1)
-    loop(1, 2, flip_group)
-    z_recv(2)
-    x_send(2)
-    loop(2, 3, flip_group)
 
     meta_copy.wait_send()
     remote(metab.at[1 - half], metab.at[1 - half], msem, 0, other).wait_recv()
@@ -149,6 +148,22 @@
     weight = jnp.concatenate(weight, axis=0)
     item_at = lax.broadcasted_iota(jnp.int32, (TILE, 128), 0).astype(F32)
 
+    vt[...] = jnp.zeros(vt.shape, F32)
+
+    def aim_group(g):
+        for u in range(GROUP):
+            here = aim - ((g * GROUP + u) * TILE).astype(F32)
+            for q in range(8):
+                aimed = item_at == here[q:q + 1, :]
+                obuf[u * TILE:(u + 1) * TILE, q * 128:(q + 1) * 128] = jnp.where(aimed, 1.0, 0.0).astype(BF16)
+        vt[...] += jnp.dot(tab_t[g], obuf[...], preferred_element_type=F32)
+
+    for piece in range(1, len(PIECES)):
+        loop(2 * piece - 2, min(2 * piece, n_group), aim_group)
+        z_recv(piece)
+        x_send(piece)
+    loop(min(2 * len(PIECES) - 2, n_group), n_group, aim_group)
+
     def unpack(piece, v):
         for s in range(*PIECES[piece]):
             part = hb[v, s].astype(F32)
@@ -167,44 +182,29 @@
         places = []
         for s in range(*PIECES[piece]):
             q = (qm + REACH[s]) % 8
-            ht[q] = hf[s].T.astype(BF16)
-            q_aim = metab[q % 2, pl.ds(8 + q // 2, 1), :] - aim_base
-            places.append((q, (q % 2) * 2 + q // 4, q_aim))
-
-        def score_group(g, carry):
-            carry = list(carry)
-            for u in range(GROUP):
-                t = g * GROUP + u
-                items = tab[pl.ds(pl.multiple_of(t * TILE, TILE), TILE), :]
-                for at, (q, side, q_aim) in enumerate(places):
-                    old, total, hit = carry[at]
-                    s = jnp.dot(items, ht[q], preferred_element_type=F32)
-                    top = jnp.max(s, axis=0, keepdims=True)
-                    e = jnp.exp(s - top)
-                    pbuf[q, t] = e
-                    top = top + bias[side, pl.ds((t + half) // 2, 1), :]
-                    mt[t, pl.ds(q, 1), :] = top
-                    new = jnp.maximum(old, top)
-                    total = total * jnp.exp(old - new) + jnp.sum(e, axis=0, keepdims=True) * jnp.exp(top - new)
-                    here = q_aim - (t * TILE).astype(F32)
-                    hit = hit + jnp.sum(jnp.where(item_at == here, s, 0.0), axis=0, keepdims=True)
-                    carry[at] = (new, total, hit)
-            return tuple(carry)
-
-        zero = jnp.zeros((1, 128), F32)
-        done = lax.fori_loop(0, n_group, score_group, tuple((zero + NEGATIVE, zero, zero) for _ in places))
-        for (q, _, _), (top, total, hit) in zip(places, done):
+            flat = hf[s].T.astype(BF16)
+            ht[q] = flat
+            hw[:, len(places) * 128:(len(places) + 1) * 128] = flat
+            places.append((q, (q % 2) * 2 + q // 4))
+        scores = jnp.dot(tab[...], hw[:, 0:len(places) * 128], preferred_element_type=F32)
+        tops = [[] for _ in places]
+        sums = [[] for _ in places]
+        for t in range(n_tile):
+            for at, (q, side) in enumerate(places):
+                s = scores[t * TILE:(t + 1) * TILE, at * 128:(at + 1) * 128]
+                top = jnp.max(s, axis=0, keepdims=True)
+                e = jnp.exp(s - top)
+                pbuf[q, t] = e
+                top = top + bias[side, pl.ds((t + half) // 2, 1), :]
+                mt[t, pl.ds(q, 1), :] = top
+                tops[at].append(top)
+                sums[at].append(jnp.sum(e, axis=0, keepdims=True))
+        for at, (q, side) in enumerate(places):
+            top = functools.reduce(jnp.maximum, tops[at])
             stx[xy, pl.ds(q, 1), :] = top
-            stx[xy, pl.ds(8 + q, 1), :] = total
-            stx[xy, pl.ds(16 + q, 1), :] = hit
-
-    score(0)
-    z_recv(3)
-    x_send(3)
-    z_recv(4)
-    x_send(4)
-    loop(3, n_group, flip_group)
-    for piece in range(1, 5):
+            stx[xy, pl.ds(8 + q, 1), :] = sum(n * jnp.exp(m - top) for n, m in zip(sums[at], tops[at]))
+
+    for piece in range(len(PIECES)):
         score(piece)
 
     def sx_copy(hits, j, v_from, v_to):
@@ -216,9 +216,12 @@
         return remote(ref, ref, hzsem if hits else szsem, j, z_dev(q_to))
 
     loop(1, 16, lambda j: sx_copy(False, j, xy, (xy + j) % 16).start())
+    top_here = stx[xy, 0:8, :]
+    for q in range(8):
+        at = slice(q * 128, (q + 1) * 128)
+        stx[xy, 16 + q:17 + q, :] = jnp.sum(ht[q].astype(F32) * vt[:, at], axis=0, keepdims=True)
+    hit_here = stx[xy, 16:24, :]
     loop(1, 16, lambda j: sx_copy(True, j, xy, (xy + j) % 16).start())
-    top_here = stx[xy, 0:8, :]
-    hit_here = stx[xy, 16:24, :]
 
     for rel in range(8):
         to = (par + (rel // 2) % 2) % 2 + 2 * ((half + rel % 2) % 2)
@@ -227,7 +230,6 @@
             hp[rel * 32:(rel + 1) * 32, q * 128:(q + 1) * 128] = ht[q, pl.ds(f0, 32), :]
 
     ut[...] = jnp.zeros(ut.shape, F32)
-    vt[...] = jnp.zeros(vt.shape, F32)
 
     def early_group(g):
         for u in range(GROUP):
@@ -238,9 +240,7 @@
                 at = slice(q * 128, (q + 1) * 128)
                 aimed = item_at == here[q:q + 1, :]
                 cbuf[u * TILE:(u + 1) * TILE, at] = jnp.where(aimed, 0.0, pbuf[q, t] * factor[q:q + 1, :]).astype(BF16)
-                obuf[u * TILE:(u + 1) * TILE, at] = jnp.where(aimed, 1.0, 0.0).astype(BF16)
         ut[...] += jnp.dot(tab_t[g], cbuf[...], preferred_element_type=F32)
-        vt[...] += jnp.dot(tab_t[g], obuf[...], preferred_element_type=F32)
 
     loop(0, EARLY, early_group)
 
@@ -276,17 +276,31 @@
     stz[qm, 8:16, :] = total
     for j in (4, 3, 5, 2, 6, 1, 7):
         sz_copy(False, j, qm, (qm + j) % 8).start()
+    loop(EARLY, n_group, early_group)
     sx_wait(True)
     stz[qm, 16:24, :] = sum_hits(stx, 16)
     for j in (4, 3, 5, 2, 6, 1, 7):
         sz_copy(True, j, qm, (qm + j) % 8).start()
-    loop(EARLY, n_group, early_group)
+
+    def x_sent(j):
+        v = (xy + j) % 16
+        for piece in range(len(PIECES)):
+            x_copy(piece, xy, v, j).wait_send()
+        sx_copy(False, j, xy, v).wait_send()
+        sx_copy(True, j, xy, v).wait_send()
+
+    loop(1, 16, x_sent)
+    for j in range(1, 8):
+        q = (qm + j) % 8
+        remote(hb.at[xy, 0], hb.at[xy, REACH.index(8 - j)], zsem, 8 - j, z_dev(q)).wait_send()
+        sz_copy(False, j, qm, q).wait_send()
+        sz_copy(True, j, qm, q).wait_send()
     sz_wait(False)
     top, total = merge(stz, 8)
     scale = weight / total
 
     def a_step(t):
-        remote(a_recv.at[t], a_recv.at[t], asem, t, sibling).wait_recv()
+        remote(a_send.at[t], a_recv.at[t], asem, t, sibling).wait()
         summed = a_keep[t] + a_recv[t].astype(F32)
         b_send[t] = summed[64:].astype(BF16)
         b_keep[t] = summed[:64]
@@ -296,7 +310,7 @@
         return pl.ds(pl.multiple_of(which * n_half + t * TILE, TILE), TILE)
 
     def b_step(t):
-        remote(b_recv.at[t], b_recv.at[t], bsem, t, partner).wait_recv()
+        remote(b_send.at[t], b_recv.at[t], bsem, t, partner).wait()
         summed = (b_keep[t] + b_recv[t].astype(F32)).astype(BF16)
         c_send[t] = summed[32:]
         gt_out[:, columns(half, t)] = summed[:32]
@@ -322,7 +336,7 @@
         def _():
             b_step(t - LAG_CHIP)
 
-    loop(0, LAG_CORE, grad_tile)
+    loop(0, HIDDEN_AT, grad_tile)
 
     on_here = (aim >= 0.0) & (aim < float(n_half))
     chance = jnp.exp(jnp.where(on_here, hit_here, NEGATIVE) - top) / total
@@ -344,17 +358,20 @@
 
     loop(1, 16, g_send)
     mine = gather_rows(xy)
-    loop(LAG_CORE, n_tile, grad_tile)
+    loop(HIDDEN_AT, n_tile, grad_tile)
     loop(n_tile - LAG_CORE, n_tile, a_step)
-
     def gx_recv(j, total):
         v = (xy + 16 - j) % 16
         remote(gr.at[v], gr.at[v], gxsem, j, xy_dev(v)).wait_recv()
+        to = (xy + j) % 16
+        remote(gs.at[to], gr.at[xy], gxsem, j, xy_dev(to)).wait_send()
         return total + gr[v].astype(F32)
 
     summed = lax.fori_loop(1, 16, gx_recv, mine)
     for q in range(8):
-        zs[q] = summed[q * 8:(q + 1) * 8, :]
+        part = summed[q * 8:(q + 1) * 8, :]
+        zs[q] = jnp.concatenate([part[:, :128], part[:, 128:]], axis=0).astype(BF16)
+        zk[q] = part
     for j in (4, 3, 5, 2, 6, 1, 7):
         remote(zs.at[(qm + j) % 8], zr.at[qm], gzsem, j, z_dev((qm + j) % 8)).start()
     loop(n_tile - LAG_CHIP, n_tile, b_step)
@@ -365,36 +382,23 @@
     line = jnp.sum(jnp.where(bucket_is_own, loss_all, 0.0), axis=0, keepdims=True)
     loss[...] = pltpu.roll(jnp.broadcast_to(line, (8, 128)), (128 - xy * 8) % 128, 1)
 
-    grad = zs[qm]
+    grad = zk[qm]
     for j in range(1, 8):
         q = (qm + 8 - j) % 8
         remote(zr.at[q], zr.at[q], gzsem, j, z_dev(q)).wait_recv()
-        grad = grad + zr[q]
+        part = zr[q].astype(F32)
+        grad = grad + jnp.concatenate([part[:8], part[8:]], axis=1)
     gh_out[...] = grad.astype(BF16)
 
     for j in range(1, 8):
         q = (qm + j) % 8
-        remote(hb.at[xy, 0], hb.at[xy, REACH.index(8 - j)], zsem, 8 - j, z_dev(q)).wait_send()
-        sz_copy(False, j, qm, q).wait_send()
-        sz_copy(True, j, qm, q).wait_send()
         remote(zs.at[q], zr.at[qm], gzsem, j, z_dev(q)).wait_send()
 
-    def x_sent(j):
-        v = (xy + j) % 16
-        for piece in range(5):
-            x_copy(piece, xy, v, j).wait_send()
-        sx_copy(False, j, xy, v).wait_send()
-        sx_copy(True, j, xy, v).wait_send()
-        remote(gs.at[v], gr.at[xy], gxsem, j, xy_dev(v)).wait_send()
-
     def t_sent(t):
-        remote(a_send.at[t], a_recv.at[t], asem, t, sibling).wait_send()
-        remote(b_send.at[t], b_recv.at[t], bsem, t, partner).wait_send()
         remote(c_send.at[t], gt_out.at[:, columns(half, t)], csem, t, other).wait_send()
         into = gt_out.at[:, columns(1 - half, t)]
         remote(c_send.at[t], into, csem, t, other).wait_recv()
 
-    loop(1, 16, x_sent)
     loop(0, n_tile, t_sent)
 
 
@@ -427,6 +431,7 @@
         vmem((16, 8, 16, 128), BF16),
         vmem((8, 128, feat), F32),
         vmem((8, feat, 128), BF16),
+        vmem((feat, 128 * max(hi - lo for lo, hi in PIECES)), BF16),
         vmem((feat, rows), BF16),
         vmem((2, 16, 128), F32),
         vmem((4, 8, 128), F32),
@@ -440,8 +445,9 @@
         vmem((feat, rows), F32),
         vmem((16, 64, feat), BF16),
         vmem((16, 64, feat), BF16),
+        vmem((8, 16, 128), BF16),
         vmem((8, 8, feat), F32),
-        vmem((8, 8, feat), F32),
+        vmem((8, 16, 128), BF16),
         vmem((n_tile, 128, TILE), BF16),
         vmem((n_tile, 128, TILE), F32),
         vmem((n_tile, 128, TILE), BF16),
@@ -453,7 +459,7 @@
         dma((4,)),
         dma((2, 1)),
         dma((2, 8)),
-        dma((2, 80)),
+        dma((2, 16 * len(PIECES))),
         dma((2, 16)),
         dma((2, 8)),
         dma((2, 16)),

time: 80.4 us -> 75.4 us (0.938)
  Pallas kernels: 78.3 us -> 73.8 us
    pallas_call x1, Pallas kernels: 76 us -> 71.4 us  [on_device(): pl.pallas_call(kernel, out_shape=(jax.ShapeDtypeStruct((8, 128), F32), gh...]
where the time goes in v3:
time: 75.4 us; the launch traced here: 74.4 us
  Pallas kernels  73.8 us (98%)
    pallas_call x1, Pallas kernels, on_device(): pl.pallas_call(kernel, out_shape=(jax.ShapeDtypeStruct((8, 128), F32), gh...  71.4 us
    pallas_call x1, Pallas kernels, on_device(): pl.pallas_call(finish, out_shape=(jax.ShapeDtypeStruct((hidden.shape[0],)...  2.36 us

profile of v3, /device:TPU:6, one launch (start us, length us, event | category | flops | bytes accessed | tf_op | source)
XLA Modules:
  0.0 74.4 jit_solution(12451402806946063623)
XLA Ops:
  0.6 71.4 %shard_map.76 = (f32[8,128]{1,0:T(8,128)}, bf16[8,256]{1,0:T(8,128)(2,1)}, bf16[32,7680]{1,0:T(8,128)(2,1)}) custom-call(bf16[8,256]{1,0:T(8,128)(2,1)} %hid_hbm.1, s32[8,128]{1,0:T(8,128)} %lists_hbm.1, s32[4,128]{1,0:T(4,128)} %bitcast.2, f32[4,128]{1,0:T(4,128)} %bitcast.3, bf16[7680,256]{1,0:T(8,128)(2,1)} %table.1), custom_call_target="tpu_custom_call" | custom-call | tf_op jit(solution)/shard_map/pallas_call | solution.py:478
  72.1 2.4 %shard_map.77 = (f32[8]{0:T(128)}, bf16[8,256]{1,0:T(8,128)(2,1)}, bf16[32,7680]{1,0:T(8,128)(2,1)}) custom-call(f32[8,128]{1,0:T(8,128)} %get-tuple-element.6.loss, bf16[8,256]{1,0:T(8,128)(2,1)} %get-tuple-element.7.gh, bf16[32,7680]{1,0:T(8,128)(2,1)} %get-tuple-element.8.gt), custom_call_target="tpu_custom_call" | custom-call | tf_op jit(solution)/shard_map/pallas_call | solution.py:487

commit v4 on v3

--- a/solution.py
+++ b/solution.py
@@ -15,9 +15,9 @@
 NEGATIVE = -1e30
 TILE = 256
 GROUP = 3
-LAG_CORE = 4
-LAG_CHIP = 9
-HIDDEN_AT = 2
+LAG_CORE = 1
+LAG_CHIP = 3
+HIDDEN_AT = 1
 EARLY = 2
 REACH = (0, 1, 7, 2, 6, 3, 5, 4)
 PIECES = ((0, 3), (3, 5), (5, 8))
@@ -307,7 +307,7 @@
         remote(b_send.at[t], b_recv.at[t], bsem, t, partner).start()
 
     def columns(which, t):
-        return pl.ds(pl.multiple_of(which * n_half + t * TILE, TILE), TILE)
+        return pl.ds(pl.multiple_of(which * n_half + t * GROUP * TILE, TILE), GROUP * TILE)
 
     def b_step(t):
         remote(b_send.at[t], b_recv.at[t], bsem, t, partner).wait()
@@ -316,14 +316,15 @@
         gt_out[:, columns(half, t)] = summed[:32]
         remote(c_send.at[t], gt_out.at[:, columns(half, t)], csem, t, other).start()
 
-    def grad_tile(t):
-        here = aim - (t * TILE).astype(F32)
-        factor = jnp.exp(mt[t] - top) * scale
-        for q in range(8):
-            at = slice(q * 128, (q + 1) * 128)
-            less = jnp.where(item_at == here[q:q + 1, :], weight[q:q + 1, :], 0.0)
-            cbuf[0:TILE, at] = (pbuf[q, t] * factor[q:q + 1, :] - less).astype(BF16)
-        g = lax.dot_general(hp[...], cbuf[0:TILE, :], (((1,), (1,)), ((), ())), preferred_element_type=F32)
+    def grad_group(t):
+        for u in range(GROUP):
+            here = aim - ((t * GROUP + u) * TILE).astype(F32)
+            factor = jnp.exp(mt[t * GROUP + u] - top) * scale
+            for q in range(8):
+                less = jnp.where(item_at == here[q:q + 1, :], weight[q:q + 1, :], 0.0)
+                coef = pbuf[q, t * GROUP + u] * factor[q:q + 1, :] - less
+                cbuf[u * TILE:(u + 1) * TILE, q * 128:(q + 1) * 128] = coef.astype(BF16)
+        g = lax.dot_general(hp[...], cbuf[...], (((1,), (1,)), ((), ())), preferred_element_type=F32)
         a_send[t] = g[128:].astype(BF16)
         a_keep[t] = g[:128]
         remote(a_send.at[t], a_recv.at[t], asem, t, sibling).start()
@@ -336,7 +337,7 @@
         def _():
             b_step(t - LAG_CHIP)
 
-    loop(0, HIDDEN_AT, grad_tile)
+    loop(0, HIDDEN_AT, grad_group)
 
     on_here = (aim >= 0.0) & (aim < float(n_half))
     chance = jnp.exp(jnp.where(on_here, hit_here, NEGATIVE) - top) / total
@@ -358,8 +359,8 @@
 
     loop(1, 16, g_send)
     mine = gather_rows(xy)
-    loop(HIDDEN_AT, n_tile, grad_tile)
-    loop(n_tile - LAG_CORE, n_tile, a_step)
+    loop(HIDDEN_AT, n_group, grad_group)
+    loop(n_group - LAG_CORE, n_group, a_step)
     def gx_recv(j, total):
         v = (xy + 16 - j) % 16
         remote(gr.at[v], gr.at[v], gxsem, j, xy_dev(v)).wait_recv()
@@ -374,7 +375,7 @@
         zk[q] = part
     for j in (4, 3, 5, 2, 6, 1, 7):
         remote(zs.at[(qm + j) % 8], zr.at[qm], gzsem, j, z_dev((qm + j) % 8)).start()
-    loop(n_tile - LAG_CHIP, n_tile, b_step)
+    loop(n_group - LAG_CHIP, n_group, b_step)
 
     sz_wait(True)
     loss_all = top + jnp.log(total) - sum_hits(stz, 8)
@@ -399,7 +400,7 @@
         into = gt_out.at[:, columns(1 - half, t)]
         remote(c_send.at[t], into, csem, t, other).wait_recv()
 
-    loop(0, n_tile, t_sent)
+    loop(0, n_group, t_sent)
 
 
 def finish(loss, gh, gt, loss_out, gh_out, gt_out, sem):
@@ -448,13 +449,13 @@
         vmem((8, 16, 128), BF16),
         vmem((8, 8, feat), F32),
         vmem((8, 16, 128), BF16),
-        vmem((n_tile, 128, TILE), BF16),
-        vmem((n_tile, 128, TILE), F32),
-        vmem((n_tile, 128, TILE), BF16),
-        vmem((n_tile, 64, TILE), BF16),
-        vmem((n_tile, 64, TILE), F32),
-        vmem((n_tile, 64, TILE), BF16),
-        vmem((n_tile, 32, TILE), BF16),
+        vmem((n_group, 128, GROUP * TILE), BF16),
+        vmem((n_group, 128, GROUP * TILE), F32),
+        vmem((n_group, 128, GROUP * TILE), BF16),
+        vmem((n_group, 64, GROUP * TILE), BF16),
+        vmem((n_group, 64, GROUP * TILE), F32),
+        vmem((n_group, 64, GROUP * TILE), BF16),
+        vmem((n_group, 32, GROUP * TILE), BF16),
         dma,
         dma((4,)),
         dma((2, 1)),
@@ -464,9 +465,9 @@
         dma((2, 8)),
         dma((2, 16)),
         dma((2, 8)),
-        dma((2, n_tile)),
-        dma((2, n_tile)),
-        dma((2, n_tile)),
+        dma((2, n_group)),
+        dma((2, n_group)),
+        dma((2, n_group)),
         dma((2, 16)),
         dma((2, 8)),
     ]

time: 75.4 us -> 74.5 us (0.988)
  Pallas kernels: 73.8 us -> 72.5 us
    pallas_call x1, Pallas kernels: 71.4 us -> 70.1 us  [on_device(): pl.pallas_call(kernel, out_shape=(jax.ShapeDtypeStruct((8, 128), F32), gh...]
where the time goes in v4:
time: 74.5 us; the launch traced here: 73.1 us
  Pallas kernels  72.5 us (97%)
    pallas_call x1, Pallas kernels, on_device(): pl.pallas_call(kernel, out_shape=(jax.ShapeDtypeStruct((8, 128), F32), gh...  70.1 us
    pallas_call x1, Pallas kernels, on_device(): pl.pallas_call(finish, out_shape=(jax.ShapeDtypeStruct((hidden.shape[0],)...  2.36 us

profile of v4, /device:TPU:6, one launch (start us, length us, event | category | flops | bytes accessed | tf_op | source)
XLA Modules:
  0.0 73.1 jit_solution(3184559303757398962)
XLA Ops:
  0.6 70.1 %shard_map.76 = (f32[8,128]{1,0:T(8,128)}, bf16[8,256]{1,0:T(8,128)(2,1)}, bf16[32,7680]{1,0:T(8,128)(2,1)}) custom-call(bf16[8,256]{1,0:T(8,128)(2,1)} %hid_hbm.1, s32[8,128]{1,0:T(8,128)} %lists_hbm.1, s32[4,128]{1,0:T(4,128)} %bitcast.2, f32[4,128]{1,0:T(4,128)} %bitcast.3, bf16[7680,256]{1,0:T(8,128)(2,1)} %table.1), custom_call_target="tpu_custom_call" | custom-call | tf_op jit(solution)/shard_map/pallas_call | solution.py:479
  70.7 2.4 %shard_map.77 = (f32[8]{0:T(128)}, bf16[8,256]{1,0:T(8,128)(2,1)}, bf16[32,7680]{1,0:T(8,128)(2,1)}) custom-call(f32[8,128]{1,0:T(8,128)} %get-tuple-element.6.loss, bf16[8,256]{1,0:T(8,128)(2,1)} %get-tuple-element.7.gh, bf16[32,7680]{1,0:T(8,128)(2,1)} %get-tuple-element.8.gt), custom_call_target="tpu_custom_call" | custom-call | tf_op jit(solution)/shard_map/pallas_call | solution.py:488

commit v5 on v4

--- a/solution.py
+++ b/solution.py
@@ -18,7 +18,7 @@
 LAG_CORE = 1
 LAG_CHIP = 3
 HIDDEN_AT = 1
-EARLY = 2
+EARLY = 3
 REACH = (0, 1, 7, 2, 6, 3, 5, 4)
 PIECES = ((0, 3), (3, 5), (5, 8))
 

time: 74.5 us -> 74.7 us (level)
  no operation moved by 1% of the time
where the time goes in v5:
time: 74.7 us; the launch traced here: 73.3 us
  Pallas kernels  72.6 us (97%)
    pallas_call x1, Pallas kernels, on_device(): pl.pallas_call(kernel, out_shape=(jax.ShapeDtypeStruct((8, 128), F32), gh...  70.3 us
    pallas_call x1, Pallas kernels, on_device(): pl.pallas_call(finish, out_shape=(jax.ShapeDtypeStruct((hidden.shape[0],)...  2.36 us

profile of v5, /device:TPU:6, one launch (start us, length us, event | category | flops | bytes accessed | tf_op | source)
XLA Modules:
  0.0 73.3 jit_solution(75180463643888100)
XLA Ops:
  0.6 70.3 %shard_map.76 = (f32[8,128]{1,0:T(8,128)}, bf16[8,256]{1,0:T(8,128)(2,1)}, bf16[32,7680]{1,0:T(8,128)(2,1)}) custom-call(bf16[8,256]{1,0:T(8,128)(2,1)} %hid_hbm.1, s32[8,128]{1,0:T(8,128)} %lists_hbm.1, s32[4,128]{1,0:T(4,128)} %bitcast.2, f32[4,128]{1,0:T(4,128)} %bitcast.3, bf16[7680,256]{1,0:T(8,128)(2,1)} %table.1), custom_call_target="tpu_custom_call" | custom-call | tf_op jit(solution)/shard_map/pallas_call | solution.py:479
  70.9 2.4 %shard_map.77 = (f32[8]{0:T(128)}, bf16[8,256]{1,0:T(8,128)(2,1)}, bf16[32,7680]{1,0:T(8,128)(2,1)}) custom-call(f32[8,128]{1,0:T(8,128)} %get-tuple-element.6.loss, bf16[8,256]{1,0:T(8,128)(2,1)} %get-tuple-element.7.gh, bf16[32,7680]{1,0:T(8,128)(2,1)} %get-tuple-element.8.gt), custom_call_target="tpu_custom_call" | custom-call | tf_op jit(solution)/shard_map/pallas_call | solution.py:488
